TPU v7x, 32 devices: a whole 2x2x4 slice. The times are simulated.
32 devices in a mesh: groups: 2 (over y), gx: 4 (over z), gy: 2 (over x), ta: 2 (over core).
Axes of the slice: x: 2, y: 2, z: 4, core: 2. Of those that a mesh axis runs over, the one named last changes fastest.
Arguments:
- field: bfloat16 [8, 16, 128, 128, 128], P(('groups', 'ta'), None, 'gx', 'gy'), parts along dimension 0, may hold values from -6 to 6
- bypass_weight: bfloat16 [16, 16], replicated, may hold values from -1.5 to 1.5
- bypass_bias: float32 [16], replicated, may hold values from -3 to 3
- spectral_weight: float32 [96, 24, 24, 2, 16, 16], P('gx', 'gy', 'ta'), may hold values from -6 to 6
Outputs:
- plume_state: bfloat16 [8, 16, 128, 128, 128], P(('groups', 'ta'), None, 'gx', 'gy'), parts along dimension 0
There are 2 independent parts, one for each index of `groups`. A program takes and returns all parts, laid end to end along the dimension named above; an argument that names none is the same for every part. Nothing has to cross between parts.
All inputs are finite; a program needn't handle non-finite values.
Results may differ from a plain program's by a relative error of at most 0.001.
Values sent between devices are 32-bit elements; how exact they have to be, the bound alone decides.
A program may use at most 448 MiB of HBM per device.

v0:
```python
import math

import jax
import jax.numpy as jnp
from jax import lax
from jax.sharding import PartitionSpec as P

C = 16
NX = 128
NY = 128
NZ = 128
TW = 4
KX = 24
KY = 24
KZ = 24
KT = 4


full_turn = 2.0 * math.pi


def kept_freq(modes, length):
    positions = jnp.arange(modes, dtype=jnp.int32)
    return jnp.where(positions < modes // 2, positions, positions - modes + length)


def phase_angle(first_index, second_index, length):
    product = first_index[:, None] * second_index[None, :] % length
    return product.astype(jnp.float32) * (full_turn / length)


def block_table(first_index, second_index, length, orient):
    angle = phase_angle(first_index, second_index, length)
    cosine = jnp.cos(angle)
    sine = orient * jnp.sin(angle)
    real_row = jnp.stack([cosine, -sine], axis=-1)
    imag_row = jnp.stack([sine, cosine], axis=-1)
    return jnp.stack([real_row, imag_row], axis=1)


def apply_table(values, axis_freq, axis_part, phase_table):
    return jnp.tensordot(
        values, phase_table, axes=((axis_freq, axis_part), (0, 1)), precision=lax.Precision.HIGHEST
    )


def contract(values, weights):
    return jnp.einsum("baiz,abzio->baoz", values, weights, precision=lax.Precision.HIGHEST)


def on_device(field, bypass_weight, bypass_bias, spectral_weight):
    time_local, channels, x_local, y_local, z_cells = field.shape
    ktx_local, ky_local, kz_local = (
        spectral_weight.shape[0],
        spectral_weight.shape[1],
        spectral_weight.shape[2],
    )
    y_piece = y_local // lax.axis_size("gx")
    z_angle = phase_angle(jnp.arange(NZ, dtype=jnp.int32), jnp.arange(KZ, dtype=jnp.int32), NZ)
    z_table = jnp.concatenate([jnp.cos(z_angle), -jnp.sin(z_angle)], axis=1)
    spectrum = jnp.dot(
        field.reshape(-1, NZ),
        z_table,
        precision=lax.Precision.HIGHEST,
        preferred_element_type=jnp.float32,
    ).reshape(time_local, C, x_local, y_local, 2, KZ)
    x_table = block_table(jnp.arange(NX, dtype=jnp.int32), kept_freq(KX, NX), NX, 1.0)
    t_table = block_table(jnp.arange(TW, dtype=jnp.int32), kept_freq(KT, TW), TW, 1.0)
    reduced_x = jnp.transpose(
        apply_table(
            lax.all_to_all(spectrum, "gx", split_axis=3, concat_axis=2, tiled=True), 2, 4, x_table
        ),
        (0, 4, 1, 2, 5, 3),
    )
    whole_time = lax.all_to_all(reduced_x, "ta", split_axis=5, concat_axis=0, tiled=True)
    reduced = jnp.transpose(apply_table(whole_time, 0, 4, t_table), (4, 0, 1, 2, 5, 3))
    flat_modes = reduced.reshape(KT * KX, C, y_piece, 2, kz_local)
    by_mode = lax.all_to_all(flat_modes, "gx", split_axis=0, concat_axis=2, tiled=True)
    y_positions = lax.axis_index("gy") * y_local + jnp.arange(y_local, dtype=jnp.int32)
    y_freqs = kept_freq(KY, NY)
    freqs = y_freqs
    y_table = block_table(y_positions, freqs, NY, 1.0)
    modes = lax.psum_scatter(
        jnp.transpose(apply_table(by_mode, 2, 3, y_table), (3, 0, 1, 4, 2)),
        "gy",
        scatter_dimension=0,
        tiled=True,
    )
    real_in = modes[:, :, :, 0, :]
    imag_in = modes[:, :, :, 1, :]
    weight_real = spectral_weight[:, :, :, 0]
    weight_imag = spectral_weight[:, :, :, 1]
    mixed_real = contract(real_in, weight_real) - contract(imag_in, weight_imag)
    mixed_imag = contract(real_in, weight_imag) + contract(imag_in, weight_real)
    mixed = jnp.stack([mixed_real, mixed_imag], axis=3)
    freqs = y_freqs
    y_inverse = block_table(freqs, y_positions, NY, -1.0)
    in_space_y = jnp.transpose(
        apply_table(lax.all_gather(mixed, "gy", axis=0, tiled=True), 0, 3, y_inverse),
        (0, 1, 3, 4, 2),
    )
    returned = lax.all_to_all(in_space_y, "gx", split_axis=2, concat_axis=0, tiled=True)
    returned = returned.reshape(KT, KX, C, y_piece, 2, kz_local)
    x_inverse = block_table(kept_freq(KX, NX), jnp.arange(NX, dtype=jnp.int32), NX, -1.0)
    t_inverse = block_table(kept_freq(KT, TW), jnp.arange(TW, dtype=jnp.int32), TW, -1.0)
    in_t = jnp.transpose(apply_table(returned, 0, 4, t_inverse), (4, 0, 1, 2, 5, 3))
    split_time = lax.all_to_all(in_t, "ta", split_axis=0, concat_axis=5, tiled=True)
    in_x = jnp.transpose(apply_table(split_time, 1, 4, x_inverse), (0, 1, 4, 2, 5, 3))
    result = lax.all_to_all(in_x, "gx", split_axis=2, concat_axis=3, tiled=True)
    back_angle = phase_angle(jnp.arange(KZ, dtype=jnp.int32), jnp.arange(NZ, dtype=jnp.int32), NZ)
    z_weight = jnp.where(jnp.arange(KZ, dtype=jnp.int32) == 0, 1.0, 2.0).astype(
        jnp.float32
    ) / float(NX * NY * NZ * TW)
    inverse_z = jnp.stack(
        [z_weight[:, None] * jnp.cos(back_angle), -z_weight[:, None] * jnp.sin(back_angle)], axis=0
    )
    spectral = jnp.tensordot(
        result, inverse_z, axes=((4, 5), (0, 1)), precision=lax.Precision.HIGHEST
    )
    bypass = jnp.einsum("tcxyz,co->toxyz", field, bypass_weight, preferred_element_type=jnp.float32)
    total = spectral + bypass + bypass_bias[None, :, None, None, None]
    return jax.nn.gelu(total, approximate=False).astype(jnp.bfloat16)


def solution(mesh):
    in_specs = (
        P(("groups", "ta"), None, "gx", "gy", None),
        P(),
        P(),
        P("gx", "gy", "ta", None, None, None),
    )
    out_specs = P(("groups", "ta"), None, "gx", "gy", None)
    return jax.shard_map(
        on_device, mesh=mesh, in_specs=in_specs, out_specs=out_specs, check_vma=False
    )
```

profile of v0, /device:TPU:0, one launch (start us, length us, event | category | flops | bytes accessed | tf_op | source)
XLA Modules:
  0.0 2370.8 jit_solution(13926376310717708143)
XLA Ops:
  45.8 45.0 %copy.132 = f32[2,16,32,64,2,24]{2,5,4,1,0,3:T(8,128)} copy(f32[2,16,32,64,2,24]{3,2,1,0,5,4:T(8,128)} %reshape.956) | data formatting | bytes 25165824 | tf_op jit(solution)/shard_map/reshape | solution.py:66
  90.8 46.9 %reshape.988 = f32[4,1,786432]{2,1,0:T(1,128)} reshape(f32[64,2,16,2,24,32]{5,4,3,2,1,0:T(8,128)} %bitcast.230) | data formatting | bytes 25165824
  145.6 273.6 %all-to-all-done = f32[4,1,786432]{2,1,0:T(1,128)} async-done(((f32[4,1,786432]{2,1,0:T(1,128)}), f32[4,1,786432]{2,1,0:T(1,128)}, u32[]{:S(2)}, u32[]{:S(2)}) %all-to-all-start) | async-done | bytes 12582944 | tf_op jit(solution)/shard_map/all_to_all | solution.py:71
  419.7 39.8 %reduce.8 = f32[4,786432]{1,0:T(4,128)} reduce(f32[4,1,786432]{2,1,0:T(1,128)} %all-to-all-done, f32[]{:T(128)} %broadcast.1293), dimensions={1}, to_apply=%all_to_all.76.reduce_sub_computation | reduce | bytes 25165828 | tf_op jit(solution)/shard_map/all_to_all | solution.py:71
  459.6 49.6 %reshape.989 = f32[64,2,16,2,24,32]{5,4,3,2,1,0:T(8,128)} reshape(f32[4,786432]{1,0:T(4,128)} %reduce.8) | data formatting | bytes 25165824
  509.2 55.8 %copy.134 = f32[2,16,4,32,16,2,24]{3,2,6,5,4,1,0:T(4,128)} copy(f32[2,16,4,32,16,2,24]{3,6,5,1,0,4,2:T(8,128)} %bitcast.231) | data formatting | bytes 25165824 | tf_op jit(solution)/shard_map/all_to_all | solution.py:71
  564.9 38.3 %reshape.958 = f32[2,16,128,16,2,24,1]{2,5,4,3,1,0,6:T(8,128)} reshape(f32[2,16,4,32,16,2,24]{3,2,6,5,4,1,0:T(4,128)} %copy.134) | data formatting | bytes 25165824 | tf_op jit(solution)/shard_map/all_to_all | solution.py:71
  624.1 27.7 %reshape.990 = f32[2,1,294912]{2,1,0:T(1,128)S(1)} reshape(f32[24,2,16,16,2,24]{5,4,3,2,1,0:T(2,128)} %bitcast.238) | data formatting | bytes 4718592
  667.2 27.7 %reshape.991 = f32[24,2,16,16,2,24]{5,4,3,2,1,0:T(2,128)} reshape(f32[2,294912]{1,0:T(2,128)S(1)} %reduce.9) | data formatting | bytes 4718592
  792.3 54.1 %all-to-all-done.2 = f32[4,1,147456]{2,1,0:T(1,128)S(1)} async-done(((f32[4,1,147456]{2,1,0:T(1,128)}), f32[4,1,147456]{2,1,0:T(1,128)S(1)}, u32[]{:S(2)}, u32[]{:S(2)}) %all-to-all-start.2) | async-done | bytes 2359328 | tf_op jit(solution)/shard_map/all_to_all | solution.py:78
  930.1 59.1 %reduce-scatter.2.cloned.1.call-done = f32[12,24,16,2,12]{1,2,4,3,0:T(8,128)} async-done(((f32[24,24,16,2,12]{1,2,4,3,0:T(8,128)}), f32[12,24,16,2,12]{1,2,4,3,0:T(8,128)}) %reduce-scatter.2.cloned.1.call-update) | async-done | bytes 442384 | tf_op jit(solution)/shard_map/reduce_scatter | solution.py:83
  1008.5 53.6 %all_gather.3 = f32[24,24,16,2,12]{1,2,4,3,0:T(8,128)S(1)} all-gather(f32[12,24,16,2,12]{1,2,4,3,0:T(8,128)S(1)} %pad_maximum_fusion), channel_id=1, replica_groups=mesh['groups'=2,'gx'=4,'gy'=2,'ta'=2] {'gy'}, dimensions={0}, use_global_device_ids=true | all-gather | bytes 1327104 | tf_op jit(solution)/shard_map/all_gather | solution.py:99
  1120.8 52.8 %all-to-all-done.3 = f32[4,1,147456]{2,1,0:T(1,128)} async-done(((f32[4,1,147456]{2,1,0:T(1,128)}), f32[4,1,147456]{2,1,0:T(1,128)}, u32[]{:S(2)}, u32[]{:S(2)}) %all-to-all-start.3) | async-done | bytes 2359328 | tf_op jit(solution)/shard_map/all_to_all | solution.py:102
  1208.6 37.0 %fusion.26 = f32[4,24,16,16,2,12]{1,0,4,5,3,2:T(4,128)S(1)} fusion(f32[24,16,4,16,2,12]{0,4,5,1,3,2:T(2,128)} %bitcast.237, f32[4,1,4,2]{0,2,1,3:T(4,128)S(1)} %copy.153, f32[4,1,4,2]{0,2,1,3:T(4,128)S(1)} %copy.152), kind=kOutput, calls=%fused_computation.42 | convolution fusion | flops 56623168 | bytes 4718848 | tf_op jit(solution)/shard_map/dot_general | solution.py:42
  1253.6 28.1 %reshape.996 = f32[2,1,294912]{2,1,0:T(1,128)S(1)} reshape(f32[4,16,16,12,2,24]{5,4,3,2,1,0:T(2,128)} %bitcast.242) | data formatting | bytes 4718592
  1297.2 27.7 %reshape.997 = f32[4,16,16,12,2,24]{5,4,3,2,1,0:T(2,128)} reshape(f32[2,294912]{1,0:T(2,128)S(1)} %reduce.12) | data formatting | bytes 4718592
  1367.1 83.9 %copy.159 = f32[2,16,128,16,2,24]{5,4,3,1,0,2:T(2,128)} copy(f32[2,16,128,16,2,24]{2,5,4,3,1,0:T(8,128)} %fusion.34) | data formatting | bytes 25165824 | tf_op jit(solution)/shard_map/transpose | solution.py:108
  1451.0 153.3 %reshape.998 = f32[4,1,786432]{2,1,0:T(1,128)} reshape(f32[128,2,16,16,2,24]{5,4,3,2,1,0:T(2,128)} %bitcast.213) | data formatting | bytes 25165824
  1633.5 251.1 %all-to-all-done.5 = f32[4,1,786432]{2,1,0:T(1,128)} async-done(((f32[4,1,786432]{2,1,0:T(1,128)}), f32[4,1,786432]{2,1,0:T(1,128)}, u32[]{:S(2)}, u32[]{:S(2)}) %all-to-all-start.5) | async-done | bytes 12582944 | tf_op jit(solution)/shard_map/all_to_all | solution.py:109
  1884.6 40.0 %reduce.13 = f32[4,786432]{1,0:T(4,128)} reduce(f32[4,1,786432]{2,1,0:T(1,128)} %all-to-all-done.5, f32[]{:T(128)} %broadcast.1293), dimensions={1}, to_apply=%all_to_all.95.reduce_sub_computation | reduce | bytes 25165828 | tf_op jit(solution)/shard_map/all_to_all | solution.py:109
  1924.6 168.8 %reshape.999 = f32[128,2,16,16,2,24]{5,4,3,2,1,0:T(2,128)} reshape(f32[4,786432]{1,0:T(4,128)} %reduce.13) | data formatting | bytes 25165824
  2093.4 98.3 %copy.160 = f32[2,16,4,32,16,2,24]{3,6,5,4,2,1,0:T(8,128)} copy(f32[2,16,4,32,16,2,24]{6,5,4,1,0,3,2:T(2,128)} %bitcast.95) | data formatting | bytes 25165824 | tf_op jit(solution)/shard_map/all_to_all | solution.py:109
  2191.7 38.6 %copy.161 = f32[2,16,32,64,2,24]{3,5,4,2,1,0:T(8,128)} copy(f32[2,16,32,64,2,24]{2,5,4,3,1,0:T(8,128)} %bitcast.229) | data formatting | bytes 25165824 | tf_op jit(solution)/shard_map/all_to_all | solution.py:109
  2230.3 133.5 %fusion.2 = bf16[2,16,32,64,128]{4,3,2,1,0:T(8,128)(2,1)} fusion(f32[16,2,32,64,128]{4,0,3,2,1:T(8,128)} %fusion.15, f32[2,16,32,64,2,24]{3,5,4,2,1,0:T(8,128)} %copy.161, f32[16]{0:T(128)S(1)} %copy-done.4, f32[2,24,128,1,1,1]{2,1,0,5,4,3:T(8,128)S(1)} %maximum_bitcast_fusion.24), kind=kOutput, calls=%fused_computation.4 | convolution fusion | flops 5393874944 | bytes 62939200 | tf_op jit(solution)/shard_map/dot_general | solution.py:117
  (74 shorter events, 472.8 us)
Async XLA Ops:
  6.5 1604.6 %copy-start = (bf16[16,16]{1,0:T(8,128)(2,1)S(1)}, bf16[16,16]{1,0:T(8,128)(2,1)}, u32[]{:S(2)}) copy-start(bf16[16,16]{1,0:T(8,128)(2,1)} %param.5) | copy-start | bytes 1540
  137.7 281.5 %all-to-all-start = ((f32[4,1,786432]{2,1,0:T(1,128)}), f32[4,1,786432]{2,1,0:T(1,128)}, u32[]{:S(2)}, u32[]{:S(2)}) async-start(f32[4,1,786432]{2,1,0:T(1,128)} %reshape.988), calls=%async_computation | async-start | bytes 25165824 | tf_op jit(solution)/shard_map/all_to_all | solution.py:71
  788.4 58.0 %all-to-all-start.2 = ((f32[4,1,147456]{2,1,0:T(1,128)}), f32[4,1,147456]{2,1,0:T(1,128)S(1)}, u32[]{:S(2)}, u32[]{:S(2)}) async-start(f32[4,1,147456]{2,1,0:T(1,128)} %reshape.992), calls=%async_computation.2 | async-start | bytes 4718592 | tf_op jit(solution)/shard_map/all_to_all | solution.py:78
  792.1 197.1 %reduce-scatter.2.cloned.1.call-start = ((), (), s32[]{:S(2)}) async-start(), calls=%async_computation.7 | async-start | bytes 7077888 | tf_op jit(solution)/shard_map/reduce_scatter | solution.py:83
  1073.0 47.5 %copy-start.3 = (f32[4,1,4,2]{2,0,3,1:T(4,128)S(1)}, f32[4,1,4,2]{2,0,3,1:T(4,128)}, u32[]{:S(2)}) copy-start(f32[4,1,4,2]{2,0,3,1:T(4,128)} %get-tuple-element.21) | copy-start | bytes 388
  1073.0 47.6 %copy-start.2 = (f32[4,1,4,2]{2,0,3,1:T(4,128)S(1)}, f32[4,1,4,2]{2,0,3,1:T(4,128)}, u32[]{:S(2)}) copy-start(f32[4,1,4,2]{2,0,3,1:T(4,128)} %get-tuple-element.22) | copy-start | bytes 388
  1115.9 57.8 %all-to-all-start.3 = ((f32[4,1,147456]{2,1,0:T(1,128)}), f32[4,1,147456]{2,1,0:T(1,128)}, u32[]{:S(2)}, u32[]{:S(2)}) async-start(f32[4,1,147456]{2,1,0:T(1,128)} %reshape.994), calls=%async_computation.4 | async-start | bytes 4718592 | tf_op jit(solution)/shard_map/all_to_all | solution.py:102
  1604.3 280.3 %all-to-all-start.5 = ((f32[4,1,786432]{2,1,0:T(1,128)}), f32[4,1,786432]{2,1,0:T(1,128)}, u32[]{:S(2)}, u32[]{:S(2)}) async-start(f32[4,1,786432]{2,1,0:T(1,128)} %reshape.998), calls=%async_computation.6 | async-start | bytes 25165824 | tf_op jit(solution)/shard_map/all_to_all | solution.py:109
  2191.7 38.6 %copy-start.4 = (f32[16]{0:T(128)S(1)}, f32[16]{0:T(128)}, u32[]{:S(2)}) copy-start(f32[16]{0:T(128)} %param.6) | copy-start | bytes 196
  2230.3 133.5 %copy-start.1 = (bf16[16,16]{1,0:T(8,128)(2,1)S(1)}, bf16[16,16]{1,0:T(8,128)(2,1)}, u32[]{:S(2)}) copy-start(bf16[16,16]{1,0:T(8,128)(2,1)} %param.5) | copy-start | bytes 1540
Sparse Core Ops, SparseCore 0:
  930.0 59.0 reduce-scatter.1
where the time goes:
time: 2390 us; the launch traced here: 2370 us
  local copies, waits for them, and re-layouts  1140 us (48%)
  waiting for transfers between devices  691 us (29%)
  matrix products  305 us (13%)
  other arithmetic  133 us (6%)
  blocking collectives  66.7 us (3%)
    unnamed x23, local copies, waits for them, and re-layouts  617 us
    all_to_all x1, waiting for transfers between devices, on_device(): lax.all_to_all(spectrum, 'gx', split_axis=3, concat_axis=2, tiled=True)  274 us
    all_to_all x1, waiting for transfers between devices, on_device(): result = lax.all_to_all(in_x, 'gx', split_axis=2, concat_axis=3, tiled=True)  251 us
    all_to_all x2, local copies, waits for them, and re-layouts, on_device(): result = lax.all_to_all(in_x, 'gx', split_axis=2, concat_axis=3, tiled=True)  137 us
    dot_general x1, matrix products, on_device(): jnp.tensordot(result, inverse_z, axes=((4, 5), (0, 1)), precision=lax.Pre...  133 us
    dot_general x6, matrix products, apply_table(): jnp.tensordot(values, phase_table, axes=((axis_freq, axis_part), (0, 1)),...  127 us
    all_to_all x3, local copies, waits for them, and re-layouts, on_device(): lax.all_to_all(spectrum, 'gx', split_axis=3, concat_axis=2, tiled=True)  94.6 us
    transpose x1, local copies, waits for them, and re-layouts, on_device(): jnp.transpose(apply_table(split_time, 1, 4, x_inverse), (0, 1, 4, 2, 5, 3))  83.9 us
  transfers between devices with their start and end apart: 5, of which 5 were waited for; matrix products, arithmetic and copies ran while one was open for 1% of the time, Pallas kernels for 0%

commit v1 on v0

v1 whole, which is shorter than its diff:
```python
import jax
import jax.numpy as jnp
import ml_dtypes
import numpy as np
from jax import lax
from jax.sharding import PartitionSpec as P

KX = 24
KY = 24
KZ = 24
KT = 4
HIGH = lax.Precision.HIGH


def kept_freq(modes, length):
    positions = np.arange(modes)
    return np.where(positions < modes // 2, positions, positions - modes + length)


def block_table(first_index, second_index, length, orient):
    angle = (first_index[:, None] * second_index[None, :] % length) * (2.0 * np.pi / length)
    cosine = np.cos(angle)
    sine = orient * np.sin(angle)
    real_row = np.stack([cosine, -sine], axis=-1)
    imag_row = np.stack([sine, cosine], axis=-1)
    return np.stack([real_row, imag_row], axis=1)


def own_part(table, axis, axis_name, size):
    start = lax.axis_index(axis_name) * size
    return lax.dynamic_slice_in_dim(jnp.asarray(table), start, size, axis=axis)


def on_device(field, bypass_weight, bypass_bias, spectral_weight):
    time_local, channels, x_local, y_local, nz = field.shape
    size_x, size_y, size_t = lax.axis_size("gx"), lax.axis_size("gy"), lax.axis_size("ta")
    nx, ny, nt = x_local * size_x, y_local * size_y, time_local * size_t
    ktx_local = spectral_weight.shape[0]
    freq_x, freq_y, freq_t = kept_freq(KX, nx), kept_freq(KY, ny), kept_freq(KT, nt)
    freq_z = np.arange(KZ)

    y_full = block_table(np.arange(ny), freq_y, ny, 1.0)[:, 0].astype(np.float32)
    y_high = y_full.astype(ml_dtypes.bfloat16)
    y_low = (y_full - y_high.astype(np.float32)).astype(ml_dtypes.bfloat16)
    in_y = sum(
        jnp.einsum(
            "tcxyz,ykp->tcxpkz",
            field,
            own_part(piece, 0, "gy", y_local),
            preferred_element_type=jnp.float32,
        )
        for piece in (y_high, y_low)
    )
    x_full = block_table(np.arange(nx), freq_x, nx, 1.0).astype(np.float32)
    in_x = jnp.einsum(
        "tcxpkz,xpmq->tcmkqz", in_y, own_part(x_full, 0, "gx", x_local), precision=HIGH
    )
    z_table = block_table(np.arange(nz), freq_z, nz, 1.0).astype(np.float32)
    in_z = jnp.einsum("tcmkqz,zqnr->tcmkrn", in_x, z_table, precision=HIGH)

    whole_time = lax.all_to_all(in_z, "ta", split_axis=5, concat_axis=0, tiled=True)
    t_table = block_table(np.arange(nt), freq_t, nt, 1.0).astype(np.float32)
    in_t = jnp.einsum("tcmkrn,trqs->kqmnsc", whole_time, t_table, precision=HIGH)
    rest = in_t.shape[3:]
    in_t = in_t.reshape((size_y, KY // size_y, KT * KX) + rest)
    by_y = lax.all_to_all(in_t, "gy", split_axis=0, concat_axis=0, tiled=True).sum(0)
    by_y = jnp.swapaxes(by_y, 0, 1).reshape((size_x, ktx_local, KY // size_y) + rest)
    modes = lax.all_to_all(by_y, "gx", split_axis=0, concat_axis=0, tiled=True).sum(0)

    real_in, imag_in = modes[:, :, :, 0, :, None], modes[:, :, :, 1, :, None]
    weight_real, weight_imag = spectral_weight[:, :, :, 0], spectral_weight[:, :, :, 1]
    mixed_real = jnp.sum(real_in * weight_real - imag_in * weight_imag, axis=3)
    mixed_imag = jnp.sum(real_in * weight_imag + imag_in * weight_real, axis=3)
    mixed = jnp.stack([mixed_real, mixed_imag], axis=3)

    gathered = lax.all_gather(mixed, "gy", axis=1, tiled=True)
    gathered = lax.all_gather(gathered, "gx", axis=0, tiled=True)
    gathered = gathered.reshape((KT, KX) + gathered.shape[1:])
    t_inverse = block_table(freq_t, np.arange(nt), nt, -1.0).astype(np.float32)
    out_t = jnp.einsum("qmknso,qstr->tomkrn", gathered, t_inverse, precision=HIGH)
    own_time = lax.all_to_all(out_t, "ta", split_axis=0, concat_axis=5, tiled=True)
    z_weight = np.where(freq_z == 0, 1.0, 2.0) / float(nx * ny * nz * nt)
    z_inverse = block_table(freq_z, np.arange(nz), nz, -1.0) * z_weight[:, None, None, None]
    out_z = jnp.einsum(
        "tomkrn,nrzp->tomkpz", own_time, z_inverse.astype(np.float32), precision=HIGH
    )
    x_inverse = block_table(freq_x, np.arange(nx), nx, -1.0).astype(np.float32)
    out_x = jnp.einsum(
        "tomkpz,mpxq->toxkqz", out_z, own_part(x_inverse, 2, "gx", x_local), precision=HIGH
    )
    y_inverse = block_table(freq_y, np.arange(ny), ny, -1.0)[:, :, :, 0].astype(np.float32)
    spectral = jnp.einsum(
        "toxkqz,kqy->toxyz", out_x, own_part(y_inverse, 2, "gy", y_local), precision=HIGH
    )
    bypass = jnp.einsum("tcxyz,co->toxyz", field, bypass_weight, preferred_element_type=jnp.float32)
    total = spectral + bypass + bypass_bias[None, :, None, None, None]
    return jax.nn.gelu(total, approximate=False).astype(jnp.bfloat16)


def solution(mesh):
    in_specs = (
        P(("groups", "ta"), None, "gx", "gy", None),
        P(),
        P(),
        P("gx", "gy", "ta", None, None, None),
    )
    out_specs = P(("groups", "ta"), None, "gx", "gy", None)
    return jax.shard_map(
        on_device, mesh=mesh, in_specs=in_specs, out_specs=out_specs, check_vma=False
    )
```

time: 2390 us -> 1300 us (0.54)
  local copies, waits for them, and re-layouts: 1140 us -> 380 us
  waiting for transfers between devices: 691 us -> 297 us
  blocking collectives: 66.7 us -> 177 us
  other arithmetic: 133 us -> 90.8 us
  matrix products: 305 us -> 331 us
    all_to_all x4 -> x0, waiting for transfers between devices: 632 us -> none  [the longest x1 274 us: on_device(): lax.all_to_all(spectrum, 'gx', split_axis=3, concat_axis=2, tiled=True)]
    unnamed x23 -> x30, local copies, waits for them, and re-layouts: 617 us -> 205 us
    all_gather x0 -> x1, waiting for transfers between devices: none -> 297 us  [on_device(): gathered = lax.all_gather(gathered, 'gx', axis=0, tiled=True)]
    all_to_all x11 -> x5, local copies, waits for them, and re-layouts: 316 us -> 73.2 us  [the longest x3 46 us: on_device(): lax.all_to_all(in_z, 'ta', split_axis=5, concat_axis=0, tiled=True)]
    all_to_all x2 -> x4, blocking collectives: 13 us -> 124 us  [the longest x1 62.6 us: on_device(): lax.all_to_all(in_t, 'gy', split_axis=0, concat_axis=0, tiled=True).sum(0)]
    transpose x5 -> x3, local copies, waits for them, and re-layouts: 124 us -> 64.6 us  [the longest x1 26.8 us: on_device(): in_z = jnp.einsum('tcmkqz,zqnr->tcmkrn', in_x, z_table, precision=HIGH)]
    reduce_scatter x1 -> x0, waiting for transfers between devices: 59.1 us -> none  [on_device(): lax.psum_scatter(jnp.transpose(apply_table(by_mode, 2, 3, y_table), (3, 0...]
    reshape x3, local copies, waits for them, and re-layouts: 80.5 us -> 29.5 us  [the longest x1 14.9 us: on_device(): in_t = in_t.reshape((size_y, KY // size_y, KT * KX) + rest)]
  transfers between devices with their start and end apart: 5 -> 1, of which waited for: 5 -> 1; matrix products, arithmetic and copies ran while one was open for 1% -> 2% of each run, Pallas kernels for 0% -> 0%
where the time goes in v1:
time: 1300 us; the launch traced here: 1290 us
  local copies, waits for them, and re-layouts  380 us (29%)
  matrix products  331 us (25%)
  waiting for transfers between devices  297 us (23%)
  blocking collectives  177 us (14%)
  other arithmetic  90.8 us (7%)
  between operations  13.8 us (1%)
    all_gather x1, waiting for transfers between devices, on_device(): gathered = lax.all_gather(gathered, 'gx', axis=0, tiled=True)  297 us
    unnamed x30, local copies, waits for them, and re-layouts  205 us
    dot_general x1, matrix products, on_device(): jnp.einsum('toxkqz,kqy->toxyz', out_x, own_part(y_inverse, 2, 'gy', y_loc...  119 us
    all_to_all x1, blocking collectives, on_device(): lax.all_to_all(in_t, 'gy', split_axis=0, concat_axis=0, tiled=True).sum(0)  62.6 us
    all_gather x1, blocking collectives, on_device(): gathered = lax.all_gather(mixed, 'gy', axis=1, tiled=True)  52.7 us
    all_to_all x3, local copies, waits for them, and re-layouts, on_device(): lax.all_to_all(in_z, 'ta', split_axis=5, concat_axis=0, tiled=True)  46 us
    all_to_all x1, blocking collectives, on_device(): lax.all_to_all(by_y, 'gx', split_axis=0, concat_axis=0, tiled=True).sum(0)  45.6 us
    dot_general x2, matrix products, on_device(): jnp.einsum('tcxyz,ykp->tcxpkz', field, own_part(piece, 0, 'gy', y_local),...  43.5 us
  transfers between devices with their start and end apart: 1, of which 1 were waited for; matrix products, arithmetic and copies ran while one was open for 2% of the time, Pallas kernels for 0%

profile of v1, /device:TPU:0, one launch (start us, length us, event | category | flops | bytes accessed | tf_op | source)
XLA Modules:
  0.0 1290.5 jit_solution(8164660480482950766)
XLA Ops:
  6.5 17.6 %fusion.31 = f32[24,2,2,16,32,128]{5,0,4,3,2,1:T(8,128)} fusion(bf16[2,16,32,64,128]{4,3,2,1,0:T(8,128)(2,1)} %param.13, bf16[128,24,2]{0,1,2:T(8,128)(2,1)} %constant.97.clone, s32[]{:T(128)S(6)} %select_n.4), kind=kOutput, calls=%fused_computation.44 | convolution fusion | flops 805306368 | bytes 41955332 | tf_op jit(solution)/shard_map/tcxyz,ykp->tcxpkz/dot_general | solution.py:46
  24.2 25.9 %add_bitcast_fusion = f32[2,16,32,2,24,128]{5,4,2,1,0,3:T(8,128)} fusion(f32[24,2,2,16,32,128]{5,0,4,3,2,1:T(8,128)} %fusion.31, bf16[2,16,32,64,128]{4,3,2,1,0:T(8,128)(2,1)} %param.13, bf16[128,24,2]{0,1,2:T(8,128)(2,1)S(1)} %copy-done.8, s32[]{:T(128)S(6)} %select_n.4), kind=kOutput, calls=%fused_computation.26 | convolution fusion | flops 811597824 | bytes 67121152 | tf_op jit(solution)/shard_map/tcxyz,ykp->tcxpkz/dot_general | solution.py:46
  50.1 25.4 %fusion.45 = f32[2,16,24,24,2,128,1]{5,2,3,1,0,4,6:T(8,128)} fusion(f32[2,16,32,2,24,128]{5,4,2,1,0,3:T(8,128)} %add_bitcast_fusion, f32[128,2,24,2]{0,2,1,3:T(8,128)S(1)} %copy-done.5, s32[]{:T(128)S(6)} %select_n.10), kind=kOutput, calls=%fused_computation.53 | convolution fusion | flops 1811939328 | bytes 44089348 | tf_op jit(solution)/shard_map/tcxpkz,xpmq->tcmkqz/dot_general | solution.py:55
  75.5 19.6 %fusion.48 = f32[2,16,24,24,2,24]{5,3,4,2,1,0:T(8,128)} fusion(f32[128,2,24,2,1,1,1]{0,2,1,3,6,5,4:T(8,128)S(1)} %copy-done.4, f32[2,16,24,24,2,128,1]{5,2,3,1,0,4,6:T(8,128)} %fusion.45), kind=kOutput, calls=%fused_computation.54 | convolution fusion | flops 1358954496 | bytes 22462464 | tf_op jit(solution)/shard_map/tcmkqz,zqnr->tcmkrn/dot_general | solution.py:59
  95.1 26.8 %copy.68 = f32[2,16,24,24,2,24]{3,4,2,1,0,5:T(2,128)} copy(f32[2,16,24,24,2,24]{5,3,4,2,1,0:T(8,128)} %fusion.48) | data formatting | bytes 7077888 | tf_op jit(solution)/shard_map/tcmkqz,zqnr->tcmkrn/transpose | solution.py:59
  121.9 46.2 %reshape.39 = f32[2,1,442368]{2,1,0:T(1,128)} reshape(f32[24,2,16,24,2,24]{5,4,3,2,1,0:T(2,128)} %bitcast.178) | data formatting | bytes 7077888
  176.5 30.4 %reduce = f32[2,442368]{1,0:T(2,128)} reduce(f32[2,1,442368]{2,1,0:T(1,128)S(1)} %all_to_all.46, f32[]{:T(128)} %broadcast.7), dimensions={1}, to_apply=%all_to_all.32.reduce_sub_computation | reduce | bytes 7077892 | tf_op jit(solution)/shard_map/all_to_all | solution.py:61
  206.9 46.3 %reshape.40 = f32[24,2,16,24,2,24]{5,4,3,2,1,0:T(2,128)} reshape(f32[2,442368]{1,0:T(2,128)} %reduce) | data formatting | bytes 7077888
  267.4 31.2 %copy.70 = f32[2,2,16,24,24,2,12]{4,1,0,5,6,3,2:T(2,128)S(1)} copy(f32[2,2,16,24,24,2,12]{4,3,6,0,5,2,1:T(8,128)} %bitcast.180) | data formatting | bytes 7077888 | tf_op jit(solution)/shard_map/all_to_all | solution.py:61
  298.6 20.4 %convolution_bitcast_fusion = f32[24,4,24,12,2,16]{0,1,4,3,2,5:T(4,128)} fusion(f32[4,16,24,24,2,12,1]{3,0,4,6,5,2,1:T(4,128)S(1)} %bitcast.176, f32[4,2,4,2,1,1,1]{0,2,1,3,6,5,4:T(4,128)S(1)} %copy-done.9), kind=kOutput, calls=%fused_computation.50 | convolution fusion | flops 42467328 | bytes 7078144 | tf_op jit(solution)/shard_map/tcmkrn,trqs->kqmnsc/dot_general | solution.py:63
  319.0 26.1 %copy.71 = f32[24,4,24,12,2,16]{2,1,5,4,3,0:T(4,128)} copy(f32[24,4,24,12,2,16]{0,1,4,3,2,5:T(4,128)} %convolution_bitcast_fusion) | data formatting | bytes 7077888 | tf_op jit(solution)/shard_map/tcmkrn,trqs->kqmnsc/transpose | solution.py:63
  360.0 62.6 %all_to_all.47 = f32[2,12,96,12,2,16]{2,5,4,3,1,0:T(8,128)} all-to-all(f32[2,12,96,12,2,16]{2,5,4,3,1,0:T(8,128)} %reshape.12), channel_id=1, replica_groups=mesh['groups'=2,'gx'=4,'gy'=2,'ta'=2] {'gy'}, dimensions={0} | all-to-all | bytes 7077888 | tf_op jit(solution)/shard_map/all_to_all | solution.py:66
  449.9 45.6 %all_to_all.48 = f32[4,1,110592]{2,1,0:T(1,128)S(1)} all-to-all(f32[4,1,110592]{2,1,0:T(1,128)S(1)} %reshape.41), channel_id=1, replica_groups=mesh['groups'=2,'gx'=4,'gy'=2,'ta'=2] {'gx'}, dimensions={0} | all-to-all | bytes 3538944 | tf_op jit(solution)/shard_map/all_to_all | solution.py:68
  533.3 52.7 %all_gather.6 = f32[24,24,12,2,16]{0,4,3,2,1:T(8,128)} all-gather(f32[24,12,12,2,16]{0,4,3,2,1:T(8,128)S(1)} %pad_maximum_fusion), channel_id=1, replica_groups=mesh['groups'=2,'gx'=4,'gy'=2,'ta'=2] {'gy'}, dimensions={1}, use_global_device_ids=true | all-gather | bytes 1327104 | tf_op jit(solution)/shard_map/all_gather | solution.py:76
  593.9 23.2 %fusion.35 = f32[16,2,32,64,128]{4,0,3,2,1:T(8,128)} fusion(bf16[2,16,32,64,128]{4,3,2,1,0:T(8,128)(2,1)} %param.13, bf16[16,16]{1,0:T(8,128)(2,1)S(1)} %copy-done), kind=kOutput, calls=%fused_computation.48 | convolution fusion | flops 268435456 | bytes 50332160 | tf_op jit(solution)/shard_map/tcxyz,co->toxyz/dot_general | solution.py:95
  617.2 297.3 %all-gather.2.cloned.1.call-done = f32[96,24,12,2,16]{1,4,3,2,0:T(8,128)} async-done(((f32[24,24,12,2,16]{1,4,3,2,0:T(8,128)}), f32[96,24,12,2,16]{1,4,3,2,0:T(8,128)}) %all-gather.2.cloned.1.call-update) | async-done | bytes 3538960 | tf_op jit(solution)/shard_map/all_gather | solution.py:77
  914.5 39.8 %fusion.42 = f32[4,16,24,24,2,12]{3,0,4,1,5,2:T(4,128)S(1)} fusion(f32[4,2,4,2,1,1,1]{0,2,1,3,6,5,4:T(4,128)S(1)} %copy-done.10, f32[4,24,24,12,2,16,1]{2,5,4,3,1,0,6:T(8,128)} %bitcast.185), kind=kOutput, calls=%fused_computation.52 | convolution fusion | flops 42467328 | bytes 7078144 | tf_op jit(solution)/shard_map/qmknso,qstr->tomkrn/dot_general | solution.py:80
  966.1 46.4 %reshape.43 = f32[2,1,442368]{2,1,0:T(1,128)} reshape(f32[4,24,12,16,2,24]{5,4,3,2,1,0:T(2,128)} %bitcast.181) | data formatting | bytes 7077888
  1020.4 30.3 %reduce.2 = f32[2,442368]{1,0:T(2,128)} reduce(f32[2,1,442368]{2,1,0:T(1,128)S(1)} %all_to_all.49, f32[]{:T(128)} %broadcast.7), dimensions={1}, to_apply=%all_to_all.38.reduce_sub_computation | reduce | bytes 7077892 | tf_op jit(solution)/shard_map/all_to_all | solution.py:81
  1050.8 46.0 %reshape.44 = f32[4,24,12,16,2,24]{5,4,3,2,1,0:T(2,128)} reshape(f32[2,442368]{1,0:T(2,128)} %reduce.2) | data formatting | bytes 7077888
  1096.7 19.9 %copy.78 = f32[4,16,24,24,2,12]{3,2,5,4,1,0:T(8,128)} copy(f32[4,16,24,24,2,12]{3,4,1,5,2,0:T(2,128)} %bitcast.182) | data formatting | bytes 7077888 | tf_op jit(solution)/shard_map/all_to_all | solution.py:81
  1124.0 17.9 %fusion.51 = f32[2,16,24,24,2,128]{5,3,4,2,1,0:T(8,128)} fusion(f32[24,2,128,2,1,1,1]{2,0,1,3,6,5,4:T(8,128)S(1)} %copy-done.3, f32[2,16,24,24,2,24,1]{3,2,5,4,1,0,6:T(8,128)S(1)} %bitcast.177), kind=kOutput, calls=%fused_computation.55 | convolution fusion | flops 1358954496 | bytes 22462464 | tf_op jit(solution)/shard_map/tomkrn,nrzp->tomkpz/dot_general | solution.py:84
  1141.8 22.8 %fusion.37 = f32[2,16,32,24,2,128]{5,2,3,1,0,4:T(8,128)S(1)} fusion(f32[2,16,24,24,2,128]{5,3,4,2,1,0:T(8,128)} %fusion.51, f32[24,2,128,2]{2,0,1,3:T(8,128)S(1)} %copy-done.2, s32[]{:T(128)S(6)} %select_n.10), kind=kOutput, calls=%fused_computation.51 | convolution fusion | flops 1811939328 | bytes 44089348 | tf_op jit(solution)/shard_map/tomkpz,mpxq->toxkqz/dot_general | solution.py:88
  1164.7 118.7 %fusion.2 = bf16[2,16,32,64,128]{4,3,2,1,0:T(8,128)(2,1)} fusion(f32[16,2,32,64,128]{4,0,3,2,1:T(8,128)} %fusion.35, f32[2,16,32,24,2,128]{5,2,3,1,0,4:T(8,128)S(1)} %fusion.37, f32[16]{0:T(128)S(1)} %copy-done.11, f32[24,2,64,1,1,1]{2,0,1,5,4,3:T(8,128)S(1)} %copy-done.7), kind=kOutput, calls=%fused_computation.3 | convolution fusion | flops 2977955840 | bytes 75509824 | tf_op jit(solution)/shard_map/toxkqz,kqy->toxyz/dot_general | solution.py:92
  (45 shorter events, 137.5 us)
Async XLA Ops:
  6.5 587.4 %copy-start = (bf16[16,16]{1,0:T(8,128)(2,1)S(1)}, bf16[16,16]{1,0:T(8,128)(2,1)}, u32[]{:S(2)}) copy-start(bf16[16,16]{1,0:T(8,128)(2,1)} %param.14) | copy-start | bytes 1540
  6.5 17.6 %copy-start.8 = (bf16[128,24,2]{0,1,2:T(8,128)(2,1)S(1)}, bf16[128,24,2]{0,1,2:T(8,128)(2,1)}, u32[]{:S(2)}) copy-start(bf16[128,24,2]{0,1,2:T(8,128)(2,1)} %constant.96.clone) | copy-start | bytes 36868
  6.5 908.0 %all-gather.2.cloned.1.call-start = ((), (), s32[]{:S(2)}) async-start(), calls=%async_computation.4 | async-start | bytes 23592960 | tf_op jit(solution)/shard_map/all_gather | solution.py:77
  24.2 25.9 %copy-start.5 = (f32[128,2,24,2]{0,2,1,3:T(8,128)S(1)}, f32[128,2,24,2]{0,2,1,3:T(8,128)}, u32[]{:S(2)}) copy-start(f32[128,2,24,2]{0,2,1,3:T(8,128)} %constant.98.clone) | copy-start | bytes 147460
  50.1 25.4 %copy-start.4 = (f32[128,2,24,2,1,1,1]{0,2,1,3,6,5,4:T(8,128)S(1)}, f32[128,2,24,2,1,1,1]{0,2,1,3,6,5,4:T(8,128)}, u32[]{:S(2)}) copy-start(f32[128,2,24,2,1,1,1]{0,2,1,3,6,5,4:T(8,128)} %constant.106) | copy-start | bytes 147460
  267.4 31.2 %copy-start.9 = (f32[4,2,4,2,1,1,1]{0,2,1,3,6,5,4:T(4,128)S(1)}, f32[4,2,4,2,1,1,1]{0,2,1,3,6,5,4:T(4,128)}, u32[]{:S(2)}) copy-start(f32[4,2,4,2,1,1,1]{0,2,1,3,6,5,4:T(4,128)} %constant.107) | copy-start | bytes 772
  518.1 75.1 %copy-start.6 = (f32[24,2,128]{2,0,1:T(8,128)S(1)}, f32[24,2,128]{2,0,1:T(8,128)}, u32[]{:S(2)}) copy-start(f32[24,2,128]{2,0,1:T(8,128)} %constant.104.clone) | copy-start | bytes 73732
  593.9 320.6 %copy-start.10 = (f32[4,2,4,2,1,1,1]{0,2,1,3,6,5,4:T(4,128)S(1)}, f32[4,2,4,2,1,1,1]{0,2,1,3,6,5,4:T(4,128)}, u32[]{:S(2)}) copy-start(f32[4,2,4,2,1,1,1]{0,2,1,3,6,5,4:T(4,128)} %constant.108) | copy-start | bytes 772
  1116.7 7.3 copy-start.3
  1123.9 17.9 %copy-start.2 = (f32[24,2,128,2]{2,0,1,3:T(8,128)S(1)}, f32[24,2,128,2]{2,0,1,3:T(8,128)}, u32[]{:S(2)}) copy-start(f32[24,2,128,2]{2,0,1,3:T(8,128)} %constant.103.clone) | copy-start | bytes 147460
  1141.8 22.9 %copy-start.7 = (f32[24,2,64,1,1,1]{2,0,1,5,4,3:T(8,128)S(1)}, f32[24,2,64,1,1,1]{2,0,1,5,4,3:T(8,128)}, u32[]{:S(2)}) copy-start(f32[24,2,64,1,1,1]{2,0,1,5,4,3:T(8,128)} %fusion.78) | copy-start | bytes 36868
  1141.8 22.9 %copy-start.11 = (f32[16]{0:T(128)S(1)}, f32[16]{0:T(128)}, u32[]{:S(2)}) copy-start(f32[16]{0:T(128)} %param.15) | copy-start | bytes 196
  1164.7 118.7 %copy-start.1 = (bf16[16,16]{1,0:T(8,128)(2,1)S(1)}, bf16[16,16]{1,0:T(8,128)(2,1)}, u32[]{:S(2)}) copy-start(bf16[16,16]{1,0:T(8,128)(2,1)} %param.14) | copy-start | bytes 1540
Sparse Core Ops, SparseCore 0:
  593.4 321.0 all-gather.1

commit v2 on v1

--- a/solution.py
+++ b/solution.py
@@ -31,6 +31,11 @@
     return lax.dynamic_slice_in_dim(jnp.asarray(table), start, size, axis=axis)
 
 
+def gather(block, axis_name, size):
+    copies = jnp.broadcast_to(block[None], (size,) + block.shape)
+    return lax.all_to_all(copies, axis_name, split_axis=0, concat_axis=0, tiled=True)
+
+
 def on_device(field, bypass_weight, bypass_bias, spectral_weight):
     time_local, channels, x_local, y_local, nz = field.shape
     size_x, size_y, size_t = lax.axis_size("gx"), lax.axis_size("gy"), lax.axis_size("ta")
@@ -53,15 +58,19 @@
     )
     x_full = block_table(np.arange(nx), freq_x, nx, 1.0).astype(np.float32)
     in_x = jnp.einsum(
-        "tcxpkz,xpmq->tcmkqz", in_y, own_part(x_full, 0, "gx", x_local), precision=HIGH
+        "tcxpkz,xpmq->tckmqz", in_y, own_part(x_full, 0, "gx", x_local), precision=HIGH
     )
     z_table = block_table(np.arange(nz), freq_z, nz, 1.0).astype(np.float32)
-    in_z = jnp.einsum("tcmkqz,zqnr->tcmkrn", in_x, z_table, precision=HIGH)
+    z_table = z_table.reshape(nz, 2, size_t, KZ // size_t, 2)
+    in_x = in_x.reshape(time_local, channels, KY * KX, 2, nz)
+    in_z = jnp.einsum("tcjqz,zqhnr->htrncj", in_x, z_table, precision=HIGH)
 
-    whole_time = lax.all_to_all(in_z, "ta", split_axis=5, concat_axis=0, tiled=True)
+    whole_time = lax.all_to_all(in_z, "ta", split_axis=0, concat_axis=0, tiled=True)
     t_table = block_table(np.arange(nt), freq_t, nt, 1.0).astype(np.float32)
-    in_t = jnp.einsum("tcmkrn,trqs->kqmnsc", whole_time, t_table, precision=HIGH)
-    rest = in_t.shape[3:]
+    t_table = t_table.reshape(size_t, time_local, 2, KT, 2)
+    in_t = jnp.einsum("htrncj,htrqs->qnscj", whole_time, t_table, precision=HIGH)
+    rest = in_t.shape[1:4]
+    in_t = jnp.transpose(in_t.reshape((KT,) + rest + (KY, KX)), (4, 0, 5, 1, 2, 3))
     in_t = in_t.reshape((size_y, KY // size_y, KT * KX) + rest)
     by_y = lax.all_to_all(in_t, "gy", split_axis=0, concat_axis=0, tiled=True).sum(0)
     by_y = jnp.swapaxes(by_y, 0, 1).reshape((size_x, ktx_local, KY // size_y) + rest)
@@ -73,20 +82,21 @@
     mixed_imag = jnp.sum(real_in * weight_imag + imag_in * weight_real, axis=3)
     mixed = jnp.stack([mixed_real, mixed_imag], axis=3)
 
-    gathered = lax.all_gather(mixed, "gy", axis=1, tiled=True)
-    gathered = lax.all_gather(gathered, "gx", axis=0, tiled=True)
-    gathered = gathered.reshape((KT, KX) + gathered.shape[1:])
+    gathered = gather(gather(mixed, "gx", size_x), "gy", size_y)
+    gathered = gathered.reshape((size_y, KT, KX) + mixed.shape[1:])
     t_inverse = block_table(freq_t, np.arange(nt), nt, -1.0).astype(np.float32)
-    out_t = jnp.einsum("qmknso,qstr->tomkrn", gathered, t_inverse, precision=HIGH)
-    own_time = lax.all_to_all(out_t, "ta", split_axis=0, concat_axis=5, tiled=True)
+    t_inverse = t_inverse.reshape(KT, 2, size_t, time_local, 2)
+    out_t = jnp.einsum("yqmbnso,qshtr->htrnoybm", gathered, t_inverse, precision=HIGH)
+    out_t = out_t.reshape(out_t.shape[:5] + (KY * KX,))
+    own_time = lax.all_to_all(out_t, "ta", split_axis=0, concat_axis=0, tiled=True)
     z_weight = np.where(freq_z == 0, 1.0, 2.0) / float(nx * ny * nz * nt)
     z_inverse = block_table(freq_z, np.arange(nz), nz, -1.0) * z_weight[:, None, None, None]
-    out_z = jnp.einsum(
-        "tomkrn,nrzp->tomkpz", own_time, z_inverse.astype(np.float32), precision=HIGH
-    )
+    z_inverse = z_inverse.astype(np.float32).reshape(size_t, KZ // size_t, 2, nz, 2)
+    out_z = jnp.einsum("htrnoj,hnrzp->tojpz", own_time, z_inverse, precision=HIGH)
+    out_z = out_z.reshape(time_local, channels, KY, KX, 2, nz)
     x_inverse = block_table(freq_x, np.arange(nx), nx, -1.0).astype(np.float32)
     out_x = jnp.einsum(
-        "tomkpz,mpxq->toxkqz", out_z, own_part(x_inverse, 2, "gx", x_local), precision=HIGH
+        "tokmpz,mpxq->toxkqz", out_z, own_part(x_inverse, 2, "gx", x_local), precision=HIGH
     )
     y_inverse = block_table(freq_y, np.arange(ny), ny, -1.0)[:, :, :, 0].astype(np.float32)
     spectral = jnp.einsum(

time: 1300 us -> 823 us (0.63)
  waiting for transfers between devices: 297 us -> 15.8 us
  local copies, waits for them, and re-layouts: 380 us -> 274 us
  matrix products: 331 us -> 288 us
  other arithmetic: 90.8 us -> 68.6 us
  between operations: 13.8 us -> 0.41 us
    all_gather x1 -> x0, waiting for transfers between devices: 297 us -> none  [on_device(): gathered = lax.all_gather(gathered, 'gx', axis=0, tiled=True)]
    all_to_all x5 -> x2, local copies, waits for them, and re-layouts: 73.2 us -> 17.4 us  [the longest x1 16.8 us: gather(): lax.all_to_all(copies, axis_name, split_axis=0, concat_axis=0, tiled=True)]
    unnamed x30, local copies, waits for them, and re-layouts: 205 us -> 151 us
    all_gather x1 -> x0, blocking collectives: 52.7 us -> none  [on_device(): gathered = lax.all_gather(mixed, 'gy', axis=1, tiled=True)]
    reshape x0 -> x3, local copies, waits for them, and re-layouts: none -> 52.3 us  [the longest x2 33.1 us: on_device(): in_t.reshape((KT,) + rest + (KY, KX))]
    transpose x3 -> x2, local copies, waits for them, and re-layouts: 64.6 us -> 19.7 us  [the longest x1 16.7 us: on_device(): jnp.einsum('yqmbnso,qshtr->htrnoybm', gathered, t_inverse, precision=HIGH)]
    all_to_all x2 -> x3, blocking collectives: 15.8 us -> 58.8 us  [the longest x1 43 us: gather(): lax.all_to_all(copies, axis_name, split_axis=0, concat_axis=0, tiled=True)]
    dot_general x6, matrix products: 146 us -> 104 us  [the longest x1 34.3 us: on_device(): jnp.einsum('yqmbnso,qshtr->htrnoybm', gathered, t_inverse, precision=HIGH)]
  transfers between devices with their start and end apart: 1 -> 1, of which waited for: 1 -> 1; matrix products, arithmetic and copies ran while one was open for 2% -> 3% of each run, Pallas kernels for 0% -> 0%
where the time goes in v2:
time: 823 us; the launch traced here: 818 us
  matrix products  288 us (35%)
  local copies, waits for them, and re-layouts  274 us (33%)
  blocking collectives  167 us (20%)
  other arithmetic  68.6 us (8%)
  waiting for transfers between devices  15.8 us (2%)
    unnamed x30, local copies, waits for them, and re-layouts  151 us
    dot_general x1, matrix products, on_device(): jnp.einsum('toxkqz,kqy->toxyz', out_x, own_part(y_inverse, 2, 'gy', y_loc...  119 us
    all_to_all x1, blocking collectives, on_device(): lax.all_to_all(in_t, 'gy', split_axis=0, concat_axis=0, tiled=True).sum(0)  62.6 us
    all_to_all x1, blocking collectives, on_device(): lax.all_to_all(by_y, 'gx', split_axis=0, concat_axis=0, tiled=True).sum(0)  45.6 us
    dot_general x2, matrix products, on_device(): jnp.einsum('tcxyz,ykp->tcxpkz', field, own_part(piece, 0, 'gy', y_local),...  43.4 us
    all_to_all x1, blocking collectives, gather(): lax.all_to_all(copies, axis_name, split_axis=0, concat_axis=0, tiled=True)  43 us
    all_to_all x2, other arithmetic, gather(): lax.all_to_all(copies, axis_name, split_axis=0, concat_axis=0, tiled=True)  36.3 us
    dot_general x1, matrix products, on_device(): jnp.einsum('yqmbnso,qshtr->htrnoybm', gathered, t_inverse, precision=HIGH)  34.3 us
  transfers between devices with their start and end apart: 1, of which 1 were waited for; matrix products, arithmetic and copies ran while one was open for 3% of the time, Pallas kernels for 0%

profile of v2, /device:TPU:0, one launch (start us, length us, event | category | flops | bytes accessed | tf_op | source)
XLA Modules:
  0.0 818.1 jit_solution(11889566123926796039)
XLA Ops:
  0.0 17.6 %fusion.29 = f32[24,2,2,16,32,128]{5,0,4,3,2,1:T(8,128)} fusion(bf16[2,16,32,64,128]{4,3,2,1,0:T(8,128)(2,1)} %param.13, bf16[128,24,2]{0,1,2:T(8,128)(2,1)} %constant.97.clone, s32[]{:T(128)S(6)} %select_n.4), kind=kOutput, calls=%fused_computation.43 | convolution fusion | flops 805306368 | bytes 41955332 | tf_op jit(solution)/shard_map/tcxyz,ykp->tcxpkz/dot_general | solution.py:51
  17.6 25.8 %add_bitcast_fusion = f32[2,16,32,2,24,128]{5,4,2,1,0,3:T(8,128)} fusion(f32[24,2,2,16,32,128]{5,0,4,3,2,1:T(8,128)} %fusion.29, bf16[2,16,32,64,128]{4,3,2,1,0:T(8,128)(2,1)} %param.13, bf16[128,24,2]{0,1,2:T(8,128)(2,1)S(1)} %copy-done.6, s32[]{:T(128)S(6)} %select_n.4), kind=kOutput, calls=%fused_computation.26 | convolution fusion | flops 811597824 | bytes 67121152 | tf_op jit(solution)/shard_map/tcxyz,ykp->tcxpkz/dot_general | solution.py:51
  43.4 25.4 %fusion.11 = f32[24,2,2,16,24,128,1]{5,0,6,4,3,2,1:T(8,128)} fusion(f32[2,16,32,2,24,128]{5,4,2,1,0,3:T(8,128)} %add_bitcast_fusion, f32[128,2,24,2]{0,2,1,3:T(8,128)S(1)} %copy-done.4, s32[]{:T(128)S(6)} %select_n.10), kind=kOutput, calls=%fused_computation.21 | convolution fusion | flops 1811939328 | bytes 44089348 | tf_op jit(solution)/shard_map/tcxpkz,xpmq->tckmqz/dot_general | solution.py:60
  100.0 13.6 %reshape.24 = f32[4,12,2,16,24,24]{5,4,0,1,2,3:T(8,128)} reshape(f32[4,12,2,16,576]{4,0,1,2,3:T(4,128)} %bitcast.186) | data formatting | bytes 7077888 | tf_op jit(solution)/shard_map/reshape | solution.py:73
  113.6 19.5 %copy.114 = f32[4,12,2,16,24,24]{5,0,3,2,1,4:T(4,128)} copy(f32[4,12,2,16,24,24]{5,4,0,1,2,3:T(8,128)} %reshape.24) | data formatting | bytes 7077888 | tf_op jit(solution)/shard_map/reshape | solution.py:73
  133.1 14.9 %reshape.25 = f32[2,12,96,12,2,16]{2,5,4,3,1,0:T(8,128)} reshape(f32[24,4,24,12,2,16]{2,1,5,4,3,0:T(4,128)} %bitcast.182) | data formatting | bytes 7077888 | tf_op jit(solution)/shard_map/reshape | solution.py:74
  148.0 62.6 %all_to_all.31 = f32[2,12,96,12,2,16]{2,5,4,3,1,0:T(8,128)} all-to-all(f32[2,12,96,12,2,16]{2,5,4,3,1,0:T(8,128)} %reshape.25), channel_id=1, replica_groups=mesh['groups'=2,'gx'=4,'gy'=2,'ta'=2] {'gy'}, dimensions={0} | all-to-all | bytes 7077888 | tf_op jit(solution)/shard_map/all_to_all | solution.py:75
  237.9 45.6 %all_to_all.32 = f32[4,1,110592]{2,1,0:T(1,128)S(1)} all-to-all(f32[4,1,110592]{2,1,0:T(1,128)S(1)} %reshape.53), channel_id=1, replica_groups=mesh['groups'=2,'gx'=4,'gy'=2,'ta'=2] {'gx'}, dimensions={0} | all-to-all | bytes 3538944 | tf_op jit(solution)/shard_map/all_to_all | solution.py:77
  306.5 15.0 %fusion.19 = (f32[24,12,12,16]{0,3,2,1:T(8,128)S(1)}, f32[24,12,12,16]{0,3,2,1:T(8,128)S(1)}) fusion(f32[24,12,12,2,16,16]{0,5,4,3,2,1:T(8,128)} %param.16, f32[24,12,12,16]{0,3,2,1:T(8,128)S(1)} %get-tuple-element.8, f32[24,12,12,16]{0,3,2,1:T(8,128)S(1)} %get-tuple-element.7), kind=kLoop, calls=%fused_computation.30 | loop fusion | flops 6967296 | bytes 7962624 | tf_op jit(solution)/shard_map/reduce_sum | solution.py:81
  329.8 18.5 %reshape.55 = f32[4,1,110592]{2,1,0:T(1,128)S(1)} reshape(f32[4,12,12,16,2,24]{5,4,3,2,1,0:T(2,128)} %broadcast_bitcast_fusion.1) | data formatting | bytes 3538944
  348.3 43.0 %all_to_all.33 = f32[4,1,110592]{2,1,0:T(1,128)S(1)} all-to-all(f32[4,1,110592]{2,1,0:T(1,128)S(1)} %reshape.55), channel_id=1, replica_groups=mesh['groups'=2,'gx'=4,'gy'=2,'ta'=2] {'gx'}, dimensions={0} | all-to-all | bytes 3538944 | tf_op jit(solution)/shard_map/all_to_all | solution.py:36
  397.2 19.3 %reshape.56 = f32[4,12,12,16,2,24]{5,4,3,2,1,0:T(2,128)} reshape(f32[4,110592]{1,0:T(4,128)S(1)} %reduce.1) | data formatting | bytes 3538944
  416.6 16.8 %copy.47 = f32[4,24,12,12,2,16]{1,0,4,5,3,2:T(4,128)} copy(f32[4,24,12,12,2,16]{1,4,5,3,2,0:T(2,128)} %bitcast.184) | data formatting | bytes 3538944 | tf_op jit(solution)/shard_map/all_to_all | solution.py:36
  433.4 13.6 %broadcast_bitcast_fusion = f32[2,12,12,16,2,4,24]{6,5,4,3,2,1,0:T(4,128)} fusion(f32[4,24,12,12,2,16]{1,0,4,5,3,2:T(4,128)} %copy.47), kind=kLoop, calls=%fused_computation.79 | loop fusion | bytes 5308416
  447.0 34.9 %reshape.57 = f32[2,1,442368]{2,1,0:T(1,128)} reshape(f32[2,12,12,16,2,4,24]{6,5,4,3,2,1,0:T(4,128)} %broadcast_bitcast_fusion) | data formatting | bytes 7077888
  487.3 22.3 %fusion.33 = f32[16,2,32,64,128]{4,0,3,2,1:T(8,128)} fusion(bf16[2,16,32,64,128]{4,3,2,1,0:T(8,128)(2,1)} %param.13, bf16[16,16]{1,0:T(8,128)(2,1)S(1)} %copy-done), kind=kOutput, calls=%fused_computation.47 | convolution fusion | flops 268435456 | bytes 50332160 | tf_op jit(solution)/shard_map/tcxyz,co->toxyz/dot_general | solution.py:105
  509.6 15.8 %all-to-all-done.4 = f32[2,1,442368]{2,1,0:T(1,128)S(1)} async-done(((f32[2,1,442368]{2,1,0:T(1,128)}), f32[2,1,442368]{2,1,0:T(1,128)S(1)}, u32[]{:S(2)}, u32[]{:S(2)}) %all-to-all-start.4) | async-done | bytes 3538976 | tf_op jit(solution)/shard_map/all_to_all | solution.py:36
  525.4 30.4 %reduce.2 = f32[2,442368]{1,0:T(2,128)} reduce(f32[2,1,442368]{2,1,0:T(1,128)S(1)} %all-to-all-done.4, f32[]{:T(128)} %broadcast.9), dimensions={1}, to_apply=%all_to_all.22.reduce_sub_computation | reduce | bytes 7077892 | tf_op jit(solution)/shard_map/all_to_all | solution.py:36
  555.7 38.5 %reshape.58 = f32[2,12,12,16,2,4,24]{6,5,4,3,2,1,0:T(4,128)} reshape(f32[2,442368]{1,0:T(2,128)} %reduce.2) | data formatting | bytes 7077888
  594.3 34.3 %fusion.35 = f32[2,2,2,12,16,2,12,24]{7,2,1,0,4,3,6,5:T(2,128)S(1)} fusion(f32[4,2,2,2,2,1,1,1,1]{0,4,1,3,2,8,7,6,5:T(2,128)S(1)} %copy-done.8, f32[2,12,12,16,2,4,24]{6,5,4,3,2,1,0:T(4,128)} %reshape.58), kind=kOutput, calls=%fused_computation.49 | convolution fusion | flops 42467328 | bytes 7078144 | tf_op jit(solution)/shard_map/yqmbnso,qshtr->htrnoybm/dot_general | solution.py:89
  628.5 16.7 %copy.48 = f32[2,2,2,12,16,2,12,24]{7,6,5,4,3,2,1,0:T(8,128)} copy(f32[2,2,2,12,16,2,12,24]{7,2,1,0,4,3,6,5:T(2,128)S(1)} %fusion.35) | data formatting | bytes 7077888 | tf_op jit(solution)/shard_map/yqmbnso,qshtr->htrnoybm/transpose | solution.py:89
  645.2 19.2 %reshape.27 = f32[2,2,2,12,16,576]{5,4,3,2,1,0:T(8,128)} reshape(f32[2,2,2,12,16,2,12,24]{7,6,5,4,3,2,1,0:T(8,128)} %copy.48) | data formatting | bytes 7077888 | tf_op jit(solution)/shard_map/reshape | solution.py:90
  684.6 14.4 %fusion.38 = f32[2,16,32,24,2,128]{5,2,3,1,0,4:T(8,128)S(1)} fusion(f32[2,16,24,24,2,128]{5,3,2,4,1,0:T(8,128)} %bitcast.185, f32[24,2,128,2]{2,0,1,3:T(8,128)S(1)} %copy-done.3, s32[]{:T(128)S(6)} %select_n.10), kind=kOutput, calls=%fused_computation.50 | convolution fusion | flops 1811939328 | bytes 44089348 | tf_op jit(solution)/shard_map/tokmpz,mpxq->toxkqz/dot_general | solution.py:98
  699.1 118.7 %fusion.2 = bf16[2,16,32,64,128]{4,3,2,1,0:T(8,128)(2,1)} fusion(f32[16,2,32,64,128]{4,0,3,2,1:T(8,128)} %fusion.33, f32[2,16,32,24,2,128]{5,2,3,1,0,4:T(8,128)S(1)} %fusion.38, f32[16]{0:T(128)S(1)} %copy-done.9, f32[24,2,64,1,1,1]{2,0,1,5,4,3:T(8,128)S(1)} %copy-done.5), kind=kOutput, calls=%fused_computation.3 | convolution fusion | flops 2977955840 | bytes 75509824 | tf_op jit(solution)/shard_map/toxkqz,kqy->toxyz/dot_general | solution.py:102
  (43 shorter events, 121.3 us)
Async XLA Ops:
  0.0 487.3 %copy-start = (bf16[16,16]{1,0:T(8,128)(2,1)S(1)}, bf16[16,16]{1,0:T(8,128)(2,1)}, u32[]{:S(2)}) copy-start(bf16[16,16]{1,0:T(8,128)(2,1)} %param.14) | copy-start | bytes 1540
  0.0 17.6 %copy-start.6 = (bf16[128,24,2]{0,1,2:T(8,128)(2,1)S(1)}, bf16[128,24,2]{0,1,2:T(8,128)(2,1)}, u32[]{:S(2)}) copy-start(bf16[128,24,2]{0,1,2:T(8,128)(2,1)} %constant.96.clone) | copy-start | bytes 36868
  17.6 25.8 %copy-start.4 = (f32[128,2,24,2]{0,2,1,3:T(8,128)S(1)}, f32[128,2,24,2]{0,2,1,3:T(8,128)}, u32[]{:S(2)}) copy-start(f32[128,2,24,2]{0,2,1,3:T(8,128)} %constant.98.clone) | copy-start | bytes 147460
  43.4 25.4 %copy-start.2 = (f32[128,2,2,12,2,1,1]{0,3,1,4,2,6,5:T(8,128)S(1)}, f32[128,2,2,12,2,1,1]{0,3,1,4,2,6,5:T(8,128)}, u32[]{:S(2)}) copy-start(f32[128,2,2,12,2,1,1]{0,3,1,4,2,6,5:T(8,128)} %constant.106) | copy-start | bytes 147460
  68.8 23.1 %copy-start.7 = (f32[2,2,2,4,2,1,1]{3,1,2,6,5,4,0:T(2,128)S(1)}, f32[2,2,2,4,2,1,1]{3,1,2,6,5,4,0:T(2,128)}, u32[]{:S(2)}) copy-start(f32[2,2,2,4,2,1,1]{3,1,2,6,5,4,0:T(2,128)} %constant.107) | copy-start | bytes 772
  481.8 43.5 %all-to-all-start.4 = ((f32[2,1,442368]{2,1,0:T(1,128)}), f32[2,1,442368]{2,1,0:T(1,128)S(1)}, u32[]{:S(2)}, u32[]{:S(2)}) async-start(f32[2,1,442368]{2,1,0:T(1,128)} %reshape.57), calls=%async_computation.4 | async-start | bytes 7077888 | tf_op jit(solution)/shard_map/all_to_all | solution.py:36
  509.6 84.7 %copy-start.8 = (f32[4,2,2,2,2,1,1,1,1]{0,4,1,3,2,8,7,6,5:T(2,128)S(1)}, f32[4,2,2,2,2,1,1,1,1]{0,4,1,3,2,8,7,6,5:T(2,128)}, u32[]{:S(2)}) copy-start(f32[4,2,2,2,2,1,1,1,1]{0,4,1,3,2,8,7,6,5:T(2,128)} %constant.108) | copy-start | bytes 772
  645.2 27.8 %copy-start.10 = (f32[2,12,2,128,2,1,1]{3,1,2,0,4,6,5:T(8,128)S(1)}, f32[2,12,2,128,2,1,1]{3,1,2,0,4,6,5:T(8,128)}, u32[]{:S(2)}) copy-start(f32[2,12,2,128,2,1,1]{3,1,2,0,4,6,5:T(8,128)} %constant.109) | copy-start | bytes 147460
  664.4 20.2 %copy-start.3 = (f32[24,2,128,2]{2,0,1,3:T(8,128)S(1)}, f32[24,2,128,2]{2,0,1,3:T(8,128)}, u32[]{:S(2)}) copy-start(f32[24,2,128,2]{2,0,1,3:T(8,128)} %constant.103.clone) | copy-start | bytes 147460
  684.6 14.5 %copy-start.5 = (f32[24,2,64,1,1,1]{2,0,1,5,4,3:T(8,128)S(1)}, f32[24,2,64,1,1,1]{2,0,1,5,4,3:T(8,128)}, u32[]{:S(2)}) copy-start(f32[24,2,64,1,1,1]{2,0,1,5,4,3:T(8,128)} %fusion.74) | copy-start | bytes 36868
  684.6 14.5 %copy-start.9 = (f32[16]{0:T(128)S(1)}, f32[16]{0:T(128)}, u32[]{:S(2)}) copy-start(f32[16]{0:T(128)} %param.15) | copy-start | bytes 196
  699.1 118.7 %copy-start.1 = (bf16[16,16]{1,0:T(8,128)(2,1)S(1)}, bf16[16,16]{1,0:T(8,128)(2,1)}, u32[]{:S(2)}) copy-start(bf16[16,16]{1,0:T(8,128)(2,1)} %param.14) | copy-start | bytes 1540
